TPU v7x, 32 devices: a whole 2x2x4 slice. The times are simulated.
32 devices in a mesh: frame: 4 (over z), lat: 4 (over y, core), lon: 2 (over x).
Axes of the slice: x: 2, y: 2, z: 4, core: 2. Of those that a mesh axis runs over, the one named last changes fastest.
Arguments:
- frames_in: bfloat16 [16, 32, 64, 512], P('frame', 'lat', 'lon'), may hold values from -6 to 6
- grad_out: bfloat16 [16, 32, 64, 512], P('frame', 'lat', 'lon'), may hold values from -6 to 6
- kernel: bfloat16 [49, 512], replicated, may hold values from -0.875 to 0.875
- w_qkv: bfloat16 [512, 1536], replicated, may hold values from -0.25 to 0.25
- w_out: bfloat16 [512, 512], replicated, may hold values from -0.25 to 0.25
Outputs:
- grad_input: bfloat16 [16, 32, 64, 512], P('frame', 'lat', 'lon')
- grad_proj: float32 [512, 2048], P(('frame', 'lat', 'lon'))
- grad_kernel: float32 [49, 512], replicated
All inputs are finite; a program needn't handle non-finite values.
Results may differ from a plain program's by a relative error of at most 0.0098.
Values may be sent and summed in bfloat16 or wider, within the bound.
A program may use at most 128 MiB of HBM per device.

v0:
```python
import functools
import math

import jax
import jax.numpy as jnp
from jax import lax
from jax.experimental import pallas as pl
from jax.experimental.pallas import tpu as pltpu
from jax.sharding import PartitionSpec as P

HEADS = 4
PAD = 8
LANES = 128
LIMIT = 40 * 1024 * 1024


def edges(block, width):
    count = lax.axis_size("lat")
    up = [(i, i + 1) for i in range(count - 1)]
    down = [(j, i) for i, j in up]
    rows = block.shape[1]
    low = lax.ppermute(block[:, rows - width :], "lat", up)
    high = lax.ppermute(block[:, :width], "lat", down)
    count = lax.axis_size("lon")
    up = [(i, i + 1) for i in range(count - 1)]
    down = [(j, i) for i, j in up]
    cols = block.shape[2]

    def strip(start):
        parts = [part[:, :, start : start + width] for part in (low, block, high)]
        return jnp.concatenate(parts, axis=1)

    left = lax.ppermute(strip(cols - width), "lon", up)
    right = lax.ppermute(strip(0), "lon", down)
    return low, high, left, right


def fill(scratch, centre, low, high, left, right, half):
    rows, cols = len(centre), centre[0].shape[0]
    for row in range(half):
        scratch[row, PAD : PAD + cols, :] = low[0, row].astype(jnp.float32)
        scratch[row + rows + half, PAD : PAD + cols, :] = high[0, row].astype(jnp.float32)
    for row in range(rows):
        scratch[row + half, PAD : PAD + cols, :] = centre[row].astype(jnp.float32)
    for row in range(rows + 2 * half):
        scratch[row, PAD - half : PAD, :] = left[0, row].astype(jnp.float32)
        scratch[row, PAD + cols : PAD + cols + half, :] = right[0, row].astype(jnp.float32)


def tile_rows(ref):
    if len(ref.shape) == 4:
        return [ref[0, row] for row in range(ref.shape[1])]
    return [ref[part, 0, row] for part in range(ref.shape[0]) for row in range(ref.shape[2])]


def conv_kernel(side, half, has_base, centre, low, high, left, right, weights, *rest):
    out, scratch = rest[-2], rest[-1]
    rows = tile_rows(centre)
    cols = rows[0].shape[0]
    fill(scratch, rows, low, high, left, right, half)
    count = len(rows)
    if has_base:
        totals = [rest[0][0, row].astype(jnp.float32) for row in range(count)]
    else:
        totals = [None] * count
    for col_tap in range(side):
        taps = [
            jnp.broadcast_to(weights[row_tap * side + col_tap], (8, scratch.shape[2]))
            for row_tap in range(side)
        ]
        first = PAD - half + col_tap
        for source in range(count + 2 * half):
            window = scratch[source, first : first + cols, :].reshape(cols // 8, 8, -1)
            for row_tap in range(side):
                row = source - row_tap
                if 0 <= row < count:
                    term = (window * taps[row_tap][None]).reshape(cols, -1)
                    totals[row] = term if totals[row] is None else totals[row] + term
    for row in range(count):
        value = totals[row].astype(out.dtype)
        if len(out.shape) == 4:
            out[0, row] = value
        else:
            out[row // out.shape[2], 0, row % out.shape[2]] = value


def tap_kernel(side, half, centre, low, high, left, right, grads, out, scratch, sums):
    frame = pl.program_id(1)
    rows = tile_rows(centre)
    cols = rows[0].shape[0]
    fill(scratch, rows, low, high, left, right, half)
    count = len(rows)

    @pl.when(frame == 0)
    def _():
        sums[...] = jnp.zeros_like(sums)

    wide = [row.astype(jnp.float32) for row in tile_rows(grads)]
    for col_tap in range(side):
        first = PAD - half + col_tap
        parts = [None] * side
        for source in range(count + 2 * half):
            window = scratch[source, first : first + cols, :]
            for row_tap in range(side):
                row = source - row_tap
                if 0 <= row < count:
                    term = jnp.sum((window * wide[row]).reshape(cols // 8, 8, -1), axis=0)
                    parts[row_tap] = term if parts[row_tap] is None else parts[row_tap] + term
        for row_tap in range(side):
            sums[row_tap * side + col_tap] += parts[row_tap]

    @pl.when(frame == pl.num_programs(1) - 1)
    def _():
        out[...] = jnp.sum(sums[...], axis=1)


def frame_spec(array, lanes, flip):
    if array.ndim == 4:
        shape = (1,) + array.shape[1:3] + (lanes,)
        place = lambda f, c: (f, 0, 0, c)
    else:
        shape = (array.shape[0], 1) + array.shape[2:4] + (lanes,)
        place = lambda f, c: (0, f, 0, 0, c)
    if flip:
        return pl.BlockSpec(shape, lambda c, f: place(f, c))
    return pl.BlockSpec(shape, place)


def padded_scratch(block, half, lanes):
    rows = block.shape[1] if block.ndim == 4 else block.shape[0] * block.shape[2]
    cols = block.shape[-2]
    return pltpu.VMEM((rows + 2 * half, cols + 2 * PAD, lanes), jnp.float32)


def conv_call(block, halo, weights, base, spread):
    frames = halo[0].shape[0]
    width = block.shape[-1]
    lanes = min(LANES, width)
    side = math.isqrt(weights.shape[0])
    half = side // 2
    rows = block.shape[1] if block.ndim == 4 else block.shape[0] * block.shape[2]
    cols = block.shape[-2]
    if spread is None:
        out = jax.ShapeDtypeStruct((frames, rows, cols, width), block.dtype)
    else:
        out = jax.ShapeDtypeStruct((spread, frames, rows // spread, cols, width), block.dtype)
    operands = [block, *halo]
    specs = [frame_spec(value, lanes, False) for value in operands]
    operands.append(weights.astype(jnp.float32)[:, None, :])
    specs.append(pl.BlockSpec((weights.shape[0], 1, lanes), lambda f, c: (0, 0, c)))
    if base is not None:
        operands.append(base)
        specs.append(frame_spec(base, lanes, False))
    flops = 2 * frames * rows * cols * width * weights.shape[0]
    return pl.pallas_call(
        functools.partial(conv_kernel, side, half, base is not None),
        grid=(frames, width // lanes),
        in_specs=specs,
        out_specs=frame_spec(out, lanes, False),
        out_shape=out,
        scratch_shapes=[padded_scratch(block, half, lanes)],
        compiler_params=pltpu.CompilerParams(vmem_limit_bytes=LIMIT),
        cost_estimate=pl.CostEstimate(flops=flops, bytes_accessed=4 * block.size, transcendentals=0),
    )(*operands)


def tap_call(block, halo, grads, side):
    frames, rows, cols, width = block.shape
    lanes = min(LANES, width)
    half = side // 2
    operands = [block, *halo, grads]
    flops = 2 * frames * rows * cols * width * side * side
    return pl.pallas_call(
        functools.partial(tap_kernel, side, half),
        grid=(width // lanes, frames),
        in_specs=[frame_spec(value, lanes, True) for value in operands],
        out_specs=pl.BlockSpec((side * side, lanes), lambda c, f: (0, c)),
        out_shape=jax.ShapeDtypeStruct((side * side, width), jnp.float32),
        scratch_shapes=[
            padded_scratch(block, half, lanes),
            pltpu.VMEM((side * side, 8, lanes), jnp.float32),
        ],
        compiler_params=pltpu.CompilerParams(vmem_limit_bytes=LIMIT),
        cost_estimate=pl.CostEstimate(flops=flops, bytes_accessed=4 * block.size, transcendentals=0),
    )(*operands)


def product(left, right, left_dim, right_dim):
    return lax.dot_general(
        left, right, (((left_dim,), (right_dim,)), ((), ())), preferred_element_type=jnp.float32
    )


def attend_kernel(
    heads, mixed, grads, w_qkv, w_out, token_grad, qkv_part, out_part, stacked, attended
):
    frames, cells, width = mixed.shape
    rows = frames * cells
    depth = width // heads
    scale = depth ** (-0.5)
    low = jnp.bfloat16

    @pl.when(pl.program_id(0) == 0)
    def _():
        qkv_part[...] = jnp.zeros_like(qkv_part)
        out_part[...] = jnp.zeros_like(out_part)

    tokens = mixed[...].reshape(rows, width)
    cotangents = grads[...].reshape(rows, width)
    projected = product(tokens, w_qkv[...], 1, 0).astype(low)
    grad_att = product(cotangents, w_out[...], 1, 1).astype(low)
    mine = lax.rem(lax.broadcasted_iota(jnp.int32, (rows, rows), 0), cells)
    theirs = lax.rem(lax.broadcasted_iota(jnp.int32, (rows, rows), 1), cells)
    same = mine == theirs
    for head in range(heads):
        start = head * depth
        queries = projected[:, start : start + depth]
        keys = projected[:, width + start : width + start + depth]
        values = projected[:, 2 * width + start : 2 * width + start + depth]
        grad_head = grad_att[:, start : start + depth]
        scores = product(queries, keys, 1, 1) * scale
        raised = jnp.where(same, jnp.exp(scores), 0.0)
        probs = raised / jnp.sum(raised, axis=1, keepdims=True)
        probs_low = probs.astype(low)
        attended[:, start : start + depth] = product(probs_low, values, 1, 0).astype(low)
        grad_probs = product(grad_head, values, 1, 1)
        inner = jnp.sum(probs * grad_probs, axis=1, keepdims=True)
        grad_scores = (probs * (grad_probs - inner) * scale).astype(low)
        stacked[:, start : start + depth] = product(grad_scores, keys, 1, 0).astype(low)
        stacked[:, width + start : width + start + depth] = product(
            grad_scores, queries, 0, 0
        ).astype(low)
        stacked[:, 2 * width + start : 2 * width + start + depth] = product(
            probs_low, grad_head, 0, 0
        ).astype(low)
    token_grad[...] = product(stacked[...], w_qkv[...], 1, 1).astype(low).reshape(token_grad.shape)
    qkv_part[...] += product(tokens, stacked[...], 0, 0)
    out_part[...] += product(attended[...], cotangents, 0, 0)


def attend_call(mixed, grads, w_qkv, w_out, heads):
    frames, count, width = mixed.shape
    cells = min(16, count)
    rows = frames * cells
    wide = w_qkv.shape[1]
    block = pl.BlockSpec((frames, cells, width), lambda g: (0, g, 0))

    def whole(*shape):
        return pl.BlockSpec(shape, lambda g: (0, 0))

    return pl.pallas_call(
        functools.partial(attend_kernel, heads),
        grid=(count // cells,),
        in_specs=[block, block, whole(width, wide), whole(width, width)],
        out_specs=[block, whole(width, wide), whole(width, width)],
        out_shape=[
            jax.ShapeDtypeStruct(mixed.shape, jnp.bfloat16),
            jax.ShapeDtypeStruct((width, wide), jnp.float32),
            jax.ShapeDtypeStruct((width, width), jnp.float32),
        ],
        scratch_shapes=[
            pltpu.VMEM((rows, wide), jnp.bfloat16),
            pltpu.VMEM((rows, width), jnp.bfloat16),
        ],
        compiler_params=pltpu.CompilerParams(vmem_limit_bytes=LIMIT),
    )(mixed, grads, w_qkv, w_out)


def swapped(value, axis, bit):
    count = lax.axis_size(axis)
    return lax.ppermute(value, axis, [(i, i ^ bit) for i in range(count)])


def paired_total(value, axes):
    for axis in axes:
        bit = 1
        while bit < lax.axis_size(axis):
            value = value + swapped(value, axis, bit)
            bit *= 2
    return value


def paired_scatter(value, axes, order):
    sizes = [lax.axis_size(axis) for axis in axes]
    digits = []
    for axis, size in zip(axes, sizes):
        bit = size // 2
        while bit >= 1:
            digits.append((axis, bit))
            bit //= 2
    rows, cols = value.shape
    value = value.reshape((2,) * len(digits) + (rows // math.prod(sizes), cols))
    for axis in order:
        bit = 1
        while bit < lax.axis_size(axis):
            dim = digits.index((axis, bit))
            mine = (lax.axis_index(axis) // bit) % 2
            digits.pop(dim)
            away = lax.dynamic_index_in_dim(value, 1 - mine, dim, keepdims=False)
            kept = lax.dynamic_index_in_dim(value, mine, dim, keepdims=False)
            came = swapped(away.astype(jnp.bfloat16), axis, bit)
            value = kept.astype(jnp.float32) + came.astype(jnp.float32)
            bit *= 2
    return value


def on_device(frames_in, grad_out, kernel, w_qkv, w_out):
    local_frames, tile_lat, tile_lon, width = frames_in.shape
    side = math.isqrt(kernel.shape[0])
    half = side // 2
    parts = lax.axis_size("frame")
    halo = edges(frames_in, half)
    share = tile_lat // parts
    grad_parts = grad_out.reshape(local_frames, parts, share, tile_lon, width)
    spread_grad = lax.all_to_all(grad_parts.transpose(1, 0, 2, 3, 4), "frame", 0, 0)
    mixed = conv_call(frames_in, halo, kernel, None, parts)
    spread_mixed = lax.all_to_all(mixed, "frame", 0, 0)
    clip = (parts * local_frames, share * tile_lon, width)
    token_grad, qkv_part, out_part = attend_call(
        spread_mixed.reshape(clip), spread_grad.reshape(clip), w_qkv, w_out, HEADS
    )
    grad_mixed = lax.all_to_all(token_grad.reshape(mixed.shape), "frame", 0, 0)
    kernel_part = tap_call(frames_in, halo, grad_mixed, side)
    grad_rows = grad_mixed.transpose(1, 0, 2, 3, 4).reshape(frames_in.shape)
    grad_halo = edges(grad_rows, half)
    grad_input = conv_call(grad_mixed, grad_halo, kernel[::-1], grad_out, None)
    total_cells = (
        local_frames
        * lax.axis_size("frame")
        * tile_lat
        * lax.axis_size("lat")
        * tile_lon
        * lax.axis_size("lon")
    )
    scale = total_cells ** (-0.5)
    grad_kernel = paired_total(kernel_part, ("lat", "lon", "frame")) * scale
    joined = jnp.concatenate([qkv_part, out_part], axis=1)
    grad_proj = paired_scatter(joined, ("frame", "lat", "lon"), ("lat", "lon", "frame")) * scale
    return (grad_input, grad_proj, grad_kernel)


def solution(mesh):
    in_specs = (P("frame", "lat", "lon", None), P("frame", "lat", "lon", None), P(), P(), P())
    out_specs = (P("frame", "lat", "lon", None), P(("frame", "lat", "lon"), None), P())
    return jax.shard_map(
        on_device, mesh=mesh, in_specs=in_specs, out_specs=out_specs, check_vma=False
    )
```

profile of v0, /device:TPU:1, one launch (start us, length us, event | category | flops | bytes accessed | tf_op | source)
XLA Modules:
  0.0 173.7 jit_solution(5648898815011689265)
XLA Ops:
  0.6 2.4 %copy.21 = bf16[4,4,2,32,512]{4,3,2,0,1:T(8,128)(2,1)} copy(bf16[4,4,2,32,512]{4,3,2,1,0:T(8,128)(2,1)} %bitcast.33) | data formatting | bytes 2097152 | tf_op jit(solution)/shard_map/reshape | solution.py:314
  3.1 5.6 %all-to-all-start.1 = ((bf16[4,4,2,32,512]{4,3,2,1,0:T(8,128)(2,1)}), bf16[4,4,2,32,512]{4,3,2,1,0:T(8,128)(2,1)S(1)}, u32[]{:S(2)}, u32[]{:S(2)}) async-start(bf16[4,4,2,32,512]{4,3,2,1,0:T(8,128)(2,1)} %bitcast.31), calls=%async_computation.1 | async-start | bytes 2097152 | tf_op jit(solution)/shard_map/all_to_all | solution.py:315
  8.7 4.0 %collective-permute-start = (bf16[4,3,32,512]{3,2,1,0:T(8,128)(2,1)S(1)}, bf16[4,3,32,512]{3,2,1,0:T(8,128)(2,1)S(1)}, u32[]{:S(2)}, u32[]{:S(2)}) collective-permute-start(bf16[4,3,32,512]{3,2,1,0:T(8,128)(2,1)S(1)} %get-tuple-element.16), channel_id=1, source_target_pairs={{0,2},{2,4},{4,6},{1,3},{3,5},{5,7},{8,10},{10,12},{12,14},{9,11},... | collective-permute-start | bytes 1179656 | tf_op jit(solution)/shard_map/ppermute | solution.py:22
  12.7 1.9 %collective-permute-start.1 = (bf16[4,3,32,512]{3,2,1,0:T(8,128)(2,1)S(1)}, bf16[4,3,32,512]{3,2,1,0:T(8,128)(2,1)S(1)}, u32[]{:S(2)}, u32[]{:S(2)}) collective-permute-start(bf16[4,3,32,512]{3,2,1,0:T(8,128)(2,1)S(1)} %get-tuple-element.15), channel_id=1, source_target_pairs={{2,0},{4,2},{6,4},{3,1},{5,3},{7,5},{10,8},{12,10},{14,12},{11,9},... | collective-permute-start | bytes 1179656 | tf_op jit(solution)/shard_map/ppermute | solution.py:23
  14.7 2.7 %collective-permute-done.low = bf16[4,3,32,512]{3,2,1,0:T(8,128)(2,1)S(1)} collective-permute-done((bf16[4,3,32,512]{3,2,1,0:T(8,128)(2,1)S(1)}, bf16[4,3,32,512]{3,2,1,0:T(8,128)(2,1)S(1)}, u32[]{:S(2)}, u32[]{:S(2)}) %collective-permute-start) | collective-permute-done | bytes 393248 | tf_op jit(solution)/shard_map/ppermute | solution.py:22
  17.4 4.6 %collective-permute-done.1.high = bf16[4,3,32,512]{3,2,1,0:T(8,128)(2,1)S(1)} collective-permute-done((bf16[4,3,32,512]{3,2,1,0:T(8,128)(2,1)S(1)}, bf16[4,3,32,512]{3,2,1,0:T(8,128)(2,1)S(1)}, u32[]{:S(2)}, u32[]{:S(2)}) %collective-permute-start.1) | collective-permute-done | bytes 393248 | tf_op jit(solution)/shard_map/ppermute | solution.py:23
  22.1 0.2 pad_maximum_fusion.2
  22.3 1.3 collective-permute-start.3
  23.8 4.0 %collective-permute-start.2 = (bf16[4,14,3,512]{3,2,1,0:T(4,128)(2,1)S(1)}, bf16[4,14,3,512]{3,2,1,0:T(4,128)(2,1)S(1)}, u32[]{:S(2)}, u32[]{:S(2)}) collective-permute-start(bf16[4,14,3,512]{3,2,1,0:T(4,128)(2,1)S(1)} %pad_maximum_fusion.1), channel_id=1, source_target_pairs={{0,1},{2,3},{4,5},{6,7},{8,9},{10,11},{12,13},{14,15},{16,17},{18,... | collective-permute-start | bytes 516104 | tf_op jit(solution)/shard_map/ppermute | solution.py:33
  27.9 1.2 collective-permute-done.3.right
  29.1 1.7 collective-permute-done.2.left
  30.7 9.6 %shard_map.76 = bf16[4,4,2,32,512]{4,3,2,1,0:T(8,128)(2,1)} custom-call(bf16[4,8,32,512]{3,2,1,0:T(8,128)(2,1)S(1)} %copy-done, bf16[4,3,32,512]{3,2,1,0:T(8,128)(2,1)S(1)} %collective-permute-done.low, bf16[4,3,32,512]{3,2,1,0:T(8,128)(2,1)S(1)} %collective-permute-done.1.high, bf16[4,14,3,512]{3,2,1,0:T(4,128)(2,1)S(1)} %collective-permute-done.2.left, ...), custom_call_target="tpu_custom_call" | custom-call | flops 51380224 | bytes 2097152 | tf_op jit(solution)/shard_map/pallas_call | solution.py:155
  40.3 0.7 copy-done.6
  41.0 0.7 copy-done.8
  41.6 4.8 %all-to-all-start = ((bf16[4,4,2,32,512]{4,3,2,1,0:T(8,128)(2,1)}), bf16[4,4,2,32,512]{4,3,2,1,0:T(8,128)(2,1)S(1)}, u32[]{:S(2)}, u32[]{:S(2)}) async-start(bf16[4,4,2,32,512]{4,3,2,1,0:T(8,128)(2,1)} %shard_map.76), calls=%async_computation | async-start | bytes 2097152 | tf_op jit(solution)/shard_map/all_to_all | solution.py:317
  46.5 22.1 %all-to-all-done = bf16[4,4,2,32,512]{4,3,2,1,0:T(8,128)(2,1)S(1)} async-done(((bf16[4,4,2,32,512]{4,3,2,1,0:T(8,128)(2,1)}), bf16[4,4,2,32,512]{4,3,2,1,0:T(8,128)(2,1)S(1)}, u32[]{:S(2)}, u32[]{:S(2)}) %all-to-all-start) | async-done | bytes 1048608 | tf_op jit(solution)/shard_map/all_to_all | solution.py:317
  68.6 1.4 copy-done.4
  70.0 1.0 copy-done.10
  71.0 14.7 %shard_map.77 = (bf16[16,64,512]{2,1,0:T(8,128)(2,1)S(1)}, f32[512,1536]{1,0:T(8,128)S(1)}, f32[512,512]{1,0:T(8,128)S(1)}) custom-call(bf16[16,64,512]{2,1,0:T(8,128)(2,1)S(1)} %bitcast.35, bf16[16,64,512]{2,1,0:T(8,128)(2,1)S(1)} %bitcast.34, bf16[512,1536]{1,0:T(8,128)(2,1)S(1)} %copy-done.4, bf16[512,512]{1,0:T(8,128)(2,1)S(1)} %copy-done.10), custom_call_target="tpu_custom_call" | custom-call | tf_op jit(solution)/shard_map/pallas_call | solution.py:251
  85.8 0.3 pad_maximum_fusion
  86.1 0.7 copy-done.5
  86.7 2.0 %copy-done.11 = f32[512,2048]{1,0:T(8,128)} copy-done((f32[512,2048]{1,0:T(8,128)}, f32[512,2048]{1,0:T(8,128)S(1)}, u32[]{:S(2)}) %copy-start.11) | copy-done | bytes 4194328
  88.7 1.1 fusion
  89.8 3.5 %all-to-all-start.2 = ((bf16[4,4,2,32,512]{4,3,2,1,0:T(8,128)(2,1)}), bf16[4,4,2,32,512]{4,3,2,1,0:T(8,128)(2,1)S(1)}, u32[]{:S(2)}, u32[]{:S(2)}) async-start(bf16[4,4,2,32,512]{4,3,2,1,0:T(8,128)(2,1)} %bitcast.36), calls=%async_computation.2 | async-start | bytes 2097152 | tf_op jit(solution)/shard_map/all_to_all | solution.py:322
  93.4 2.2 %bitcast_add_fusion = f32[2,2,2,2,16,2048]{5,4,0,1,3,2:T(8,128)S(1)} fusion(bf16[2,2,2,2,16,2048]{5,4,0,1,3,2:T(8,128)(2,1)} %collective-permute-done.8, f32[2,2,2,2,2,16,2048]{6,5,4,3,2,1,0:T(8,128)} %bitcast.38, s32[]{:T(128)S(6)} %select_n.69), kind=kLoop, calls=%fused_computation.2 | loop fusion | flops 1048576 | bytes 5242884 | tf_op jit(solution)/shard_map/add | solution.py:302
  95.7 1.3 copy-done.12
  97.0 0.9 fusion.1
  97.9 20.8 %all-to-all-done.2.centre.grads = bf16[4,4,2,32,512]{4,3,2,1,0:T(8,128)(2,1)S(1)} async-done(((bf16[4,4,2,32,512]{4,3,2,1,0:T(8,128)(2,1)}), bf16[4,4,2,32,512]{4,3,2,1,0:T(8,128)(2,1)S(1)}, u32[]{:S(2)}, u32[]{:S(2)}) %all-to-all-start.2) | async-done | bytes 1048608 | tf_op jit(solution)/shard_map/all_to_all | solution.py:322
  118.7 8.8 %shard_map.79 = f32[49,512]{1,0:T(8,128)S(1)} custom-call(bf16[4,8,32,512]{3,2,1,0:T(8,128)(2,1)S(1)} %copy-done, bf16[4,3,32,512]{3,2,1,0:T(8,128)(2,1)S(1)} %collective-permute-done.low, bf16[4,3,32,512]{3,2,1,0:T(8,128)(2,1)S(1)} %copy-done.3, bf16[4,14,3,512]{3,2,1,0:T(4,128)(2,1)S(1)} %copy-done.9, bf16[4,14,3,512]{3,2,1,0:T(4,128)(2,1)S(1)} %copy-done.7, ...), custom_call_target="tpu_custom_call" | custom-call | flops 51380224 | bytes 2097152 | tf_op jit(solution)/shard_map/pallas_call | solution.py:173
  127.4 1.4 collective-permute-start.13
  128.8 1.1 bitcast_add_fusion.1
  130.1 2.3 %collective-permute-start.10 = (bf16[2,2,16,2048]{3,2,0,1:T(8,128)(2,1)S(1)}, bf16[2,2,16,2048]{3,2,0,1:T(8,128)(2,1)S(1)}, u32[]{:S(2)}, u32[]{:S(2)}) collective-permute-start(bf16[2,2,16,2048]{3,2,0,1:T(8,128)(2,1)S(1)} %fusion.2), channel_id=1, source_target_pairs={{0,1},{1,0},{2,3},{3,2},{4,5},{5,4},{6,7},{7,6},{8,9},{9,8},{10,11... | collective-permute-start | bytes 786440 | tf_op jit(solution)/shard_map/ppermute | solution.py:271
  132.9 4.3 %collective-permute-done.14 = f32[49,512]{1,0:T(8,128)S(1)} collective-permute-done((f32[49,512]{1,0:T(8,128)S(1)}, f32[49,512]{1,0:T(8,128)S(1)}, u32[]{:S(2)}, u32[]{:S(2)}) %collective-permute-start.14) | collective-permute-done | bytes 100384 | tf_op jit(solution)/shard_map/ppermute | solution.py:271
  137.2 0.5 collective-permute-start.15
  137.7 1.3 collective-permute-done.10
  139.0 1.1 bitcast_add_fusion.2
  140.3 1.9 %collective-permute-start.4 = (bf16[4,3,32,512]{3,2,1,0:T(8,128)(2,1)S(1)}, bf16[4,3,32,512]{3,2,1,0:T(8,128)(2,1)S(1)}, u32[]{:S(2)}, u32[]{:S(2)}) collective-permute-start(bf16[4,3,32,512]{3,2,1,0:T(8,128)(2,1)S(1)} %get-tuple-element.12), channel_id=1, source_target_pairs={{0,2},{2,4},{4,6},{1,3},{3,5},{5,7},{8,10},{10,12},{12,14},{9,11},... | collective-permute-start | bytes 1179656 | tf_op jit(solution)/shard_map/ppermute | solution.py:22
  142.2 2.4 %collective-permute-start.5 = (bf16[4,3,32,512]{3,2,1,0:T(8,128)(2,1)S(1)}, bf16[4,3,32,512]{3,2,1,0:T(8,128)(2,1)S(1)}, u32[]{:S(2)}, u32[]{:S(2)}) collective-permute-start(bf16[4,3,32,512]{3,2,1,0:T(8,128)(2,1)S(1)} %get-tuple-element.11), channel_id=1, source_target_pairs={{2,0},{4,2},{6,4},{3,1},{5,3},{7,5},{10,8},{12,10},{14,12},{11,9},... | collective-permute-start | bytes 1179656 | tf_op jit(solution)/shard_map/ppermute | solution.py:23
  144.7 1.5 collective-permute-start.16
  146.4 0.6 collective-permute-done.4.low
  147.0 4.6 %collective-permute-done.5.high = bf16[4,3,32,512]{3,2,1,0:T(8,128)(2,1)S(1)} collective-permute-done((bf16[4,3,32,512]{3,2,1,0:T(8,128)(2,1)S(1)}, bf16[4,3,32,512]{3,2,1,0:T(8,128)(2,1)S(1)}, u32[]{:S(2)}, u32[]{:S(2)}) %collective-permute-start.5) | collective-permute-done | bytes 393248 | tf_op jit(solution)/shard_map/ppermute | solution.py:23
  151.8 1.3 collective-permute-start.7
  153.3 4.0 %collective-permute-start.6 = (bf16[4,14,3,512]{3,2,1,0:T(4,128)(2,1)S(1)}, bf16[4,14,3,512]{3,2,1,0:T(4,128)(2,1)S(1)}, u32[]{:S(2)}, u32[]{:S(2)}) collective-permute-start(bf16[4,14,3,512]{3,2,1,0:T(4,128)(2,1)S(1)} %pad_maximum_fusion.3), channel_id=1, source_target_pairs={{0,1},{2,3},{4,5},{6,7},{8,9},{10,11},{12,13},{14,15},{16,17},{18,... | collective-permute-start | bytes 516104 | tf_op jit(solution)/shard_map/ppermute | solution.py:33
  157.4 1.5 collective-permute-start.17
  158.9 0.7 fusion.4
  159.5 3.7 %collective-permute-done.17 = f32[49,512]{1,0:T(8,128)S(1)} collective-permute-done((f32[49,512]{1,0:T(8,128)S(1)}, f32[49,512]{1,0:T(8,128)S(1)}, u32[]{:S(2)}, u32[]{:S(2)}) %collective-permute-start.17) | collective-permute-done | bytes 100384 | tf_op jit(solution)/shard_map/ppermute | solution.py:271
  163.2 0.7 add_multiply_fusion
  163.9 9.8 %shard_map.78 = bf16[4,8,32,512]{3,2,1,0:T(8,128)(2,1)} custom-call(bf16[4,4,2,32,512]{4,3,2,1,0:T(8,128)(2,1)S(1)} %all-to-all-done.2.centre.grads, bf16[4,3,32,512]{3,2,1,0:T(8,128)(2,1)S(1)} %collective-permute-done.4.low, bf16[4,3,32,512]{3,2,1,0:T(8,128)(2,1)S(1)} %collective-permute-done.5.high, ...), custom_call_target="tpu_custom_call" | custom-call | flops 51380224 | bytes 2097152 | tf_op jit(solution)/shard_map/pallas_call | solution.py:155
  (65 shorter events, 1.8 us)
Async XLA Ops:
  0.6 8.0 %copy-start = (bf16[4,8,32,512]{3,2,1,0:T(8,128)(2,1)S(1)}, bf16[4,8,32,512]{3,2,1,0:T(8,128)(2,1)}, u32[]{:S(2)}) copy-start(bf16[4,8,32,512]{3,2,1,0:T(8,128)(2,1)} %centre.3) | copy-start | bytes 3145732
  3.1 24.7 %copy-start.15 = (bf16[49,512]{1,0:T(8,128)(2,1)S(1)}, bf16[49,512]{1,0:T(8,128)(2,1)}, u32[]{:S(2)}) copy-start(bf16[49,512]{1,0:T(8,128)(2,1)} %param.7) | copy-start | bytes 150532
  3.1 38.6 %all-to-all-start.1 = ((bf16[4,4,2,32,512]{4,3,2,1,0:T(8,128)(2,1)}), bf16[4,4,2,32,512]{4,3,2,1,0:T(8,128)(2,1)S(1)}, u32[]{:S(2)}, u32[]{:S(2)}) async-start(bf16[4,4,2,32,512]{4,3,2,1,0:T(8,128)(2,1)} %bitcast.31), calls=%async_computation.1 | async-start | bytes 2097152 | tf_op jit(solution)/shard_map/all_to_all | solution.py:315
  8.7 8.7 %collective-permute-start = (bf16[4,3,32,512]{3,2,1,0:T(8,128)(2,1)S(1)}, bf16[4,3,32,512]{3,2,1,0:T(8,128)(2,1)S(1)}, u32[]{:S(2)}, u32[]{:S(2)}) collective-permute-start(bf16[4,3,32,512]{3,2,1,0:T(8,128)(2,1)S(1)} %get-tuple-element.16), channel_id=1, source_target_pairs={{0,2},{2,4},{4,6},{1,3},{3,5},{5,7},{8,10},{10,12},{12,14},{9,11},... | collective-permute-start | bytes 1179656 | tf_op jit(solution)/shard_map/ppermute | solution.py:22
  12.7 9.4 %collective-permute-start.1 = (bf16[4,3,32,512]{3,2,1,0:T(8,128)(2,1)S(1)}, bf16[4,3,32,512]{3,2,1,0:T(8,128)(2,1)S(1)}, u32[]{:S(2)}, u32[]{:S(2)}) collective-permute-start(bf16[4,3,32,512]{3,2,1,0:T(8,128)(2,1)S(1)} %get-tuple-element.15), channel_id=1, source_target_pairs={{2,0},{4,2},{6,4},{3,1},{5,3},{7,5},{10,8},{12,10},{14,12},{11,9},... | collective-permute-start | bytes 1179656 | tf_op jit(solution)/shard_map/ppermute | solution.py:23
  22.1 19.6 %copy-start.2 = (bf16[4,3,32,512]{3,2,1,0:T(8,128)(2,1)}, bf16[4,3,32,512]{3,2,1,0:T(8,128)(2,1)S(1)}, u32[]{:S(2)}) copy-start(bf16[4,3,32,512]{3,2,1,0:T(8,128)(2,1)S(1)} %collective-permute-done.1.high) | copy-start | bytes 1179652
  22.3 6.8 %collective-permute-start.3 = (bf16[4,14,3,512]{3,2,1,0:T(4,128)(2,1)S(1)}, bf16[4,14,3,512]{3,2,1,0:T(4,128)(2,1)S(1)}, u32[]{:S(2)}, u32[]{:S(2)}) collective-permute-start(bf16[4,14,3,512]{3,2,1,0:T(4,128)(2,1)S(1)} %pad_maximum_fusion.2), channel_id=1, source_target_pairs={{1,0},{3,2},{5,4},{7,6},{9,8},{11,10},{13,12},{15,14},{17,16},{19,... | collective-permute-start | bytes 516104 | tf_op jit(solution)/shard_map/ppermute | solution.py:34
  23.8 7.0 %collective-permute-start.2 = (bf16[4,14,3,512]{3,2,1,0:T(4,128)(2,1)S(1)}, bf16[4,14,3,512]{3,2,1,0:T(4,128)(2,1)S(1)}, u32[]{:S(2)}, u32[]{:S(2)}) collective-permute-start(bf16[4,14,3,512]{3,2,1,0:T(4,128)(2,1)S(1)} %pad_maximum_fusion.1), channel_id=1, source_target_pairs={{0,1},{2,3},{4,5},{6,7},{8,9},{10,11},{12,13},{14,15},{16,17},{18,... | collective-permute-start | bytes 516104 | tf_op jit(solution)/shard_map/ppermute | solution.py:33
  40.3 0.7 copy-start.6
  41.0 0.7 copy-start.8
  41.6 26.9 %all-to-all-start = ((bf16[4,4,2,32,512]{4,3,2,1,0:T(8,128)(2,1)}), bf16[4,4,2,32,512]{4,3,2,1,0:T(8,128)(2,1)S(1)}, u32[]{:S(2)}, u32[]{:S(2)}) async-start(bf16[4,4,2,32,512]{4,3,2,1,0:T(8,128)(2,1)} %shard_map.76), calls=%async_computation | async-start | bytes 2097152 | tf_op jit(solution)/shard_map/all_to_all | solution.py:317
  68.6 1.4 copy-start.4
  70.0 1.0 copy-start.10
  85.8 1.0 copy-start.5
  86.7 2.0 %copy-start.11 = (f32[512,2048]{1,0:T(8,128)}, f32[512,2048]{1,0:T(8,128)S(1)}, u32[]{:S(2)}) copy-start(f32[512,2048]{1,0:T(8,128)S(1)} %pad_maximum_fusion) | copy-start | bytes 12582916
  89.8 3.6 %collective-permute-start.8 = (bf16[2,2,2,2,16,2048]{5,4,0,1,3,2:T(8,128)(2,1)}, bf16[2,2,2,2,16,2048]{5,4,0,1,3,2:T(8,128)(2,1)}, u32[]{:S(2)}, u32[]{:S(2)}) collective-permute-start(bf16[2,2,2,2,16,2048]{5,4,0,1,3,2:T(8,128)(2,1)} %fusion), channel_id=1, source_target_pairs={{0,2},{2,0},{4,6},{6,4},{1,3},{3,1},{5,7},{7,5},{8,10},{10,8},{12,... | collective-permute-start | bytes 3145736 | tf_op jit(solution)/shard_map/ppermute | solution.py:271
  89.8 28.8 %all-to-all-start.2 = ((bf16[4,4,2,32,512]{4,3,2,1,0:T(8,128)(2,1)}), bf16[4,4,2,32,512]{4,3,2,1,0:T(8,128)(2,1)S(1)}, u32[]{:S(2)}, u32[]{:S(2)}) async-start(bf16[4,4,2,32,512]{4,3,2,1,0:T(8,128)(2,1)} %bitcast.36), calls=%async_computation.2 | async-start | bytes 2097152 | tf_op jit(solution)/shard_map/all_to_all | solution.py:322
  93.4 25.3 %copy-start.3 = (bf16[4,3,32,512]{3,2,1,0:T(8,128)(2,1)S(1)}, bf16[4,3,32,512]{3,2,1,0:T(8,128)(2,1)}, u32[]{:S(2)}) copy-start(bf16[4,3,32,512]{3,2,1,0:T(8,128)(2,1)} %copy-done.2) | copy-start | bytes 1179652
  93.4 25.2 %copy-start.7 = (bf16[4,14,3,512]{3,2,1,0:T(4,128)(2,1)S(1)}, bf16[4,14,3,512]{3,2,1,0:T(4,128)(2,1)}, u32[]{:S(2)}) copy-start(bf16[4,14,3,512]{3,2,1,0:T(4,128)(2,1)} %copy-done.6) | copy-start | bytes 516100
  93.4 25.2 %copy-start.9 = (bf16[4,14,3,512]{3,2,1,0:T(4,128)(2,1)S(1)}, bf16[4,14,3,512]{3,2,1,0:T(4,128)(2,1)}, u32[]{:S(2)}) copy-start(bf16[4,14,3,512]{3,2,1,0:T(4,128)(2,1)} %copy-done.8) | copy-start | bytes 516100
  95.7 1.3 copy-start.12
  97.9 31.0 %collective-permute-start.9 = (bf16[2,2,2,16,2048]{4,3,0,1,2:T(8,128)(2,1)}, bf16[2,2,2,16,2048]{4,3,0,1,2:T(8,128)(2,1)}, u32[]{:S(2)}, u32[]{:S(2)}) collective-permute-start(bf16[2,2,2,16,2048]{4,3,0,1,2:T(8,128)(2,1)} %fusion.1), channel_id=1, source_target_pairs={{0,4},{2,6},{4,0},{6,2},{1,5},{3,7},{5,1},{7,3},{8,12},{10,14},{12... | collective-permute-start | bytes 1572872 | tf_op jit(solution)/shard_map/ppermute | solution.py:271
  97.9 34.5 %copy-start.16 = (bf16[49,512]{1,0:T(8,128)(2,1)S(1)}, bf16[49,512]{1,0:T(8,128)(2,1)}, u32[]{:S(2)}) copy-start(bf16[49,512]{1,0:T(8,128)(2,1)} %param.7) | copy-start | bytes 150532
  118.7 10.2 %copy-start.13 = (f32[2,2,2,2,16,2048]{5,4,0,1,3,2:T(8,128)S(1)}, f32[2,2,2,2,16,2048]{5,4,0,1,3,2:T(8,128)}, u32[]{:S(2)}) copy-start(f32[2,2,2,2,16,2048]{5,4,0,1,3,2:T(8,128)} %copy-done.12) | copy-start | bytes 6291460
  127.4 5.3 %collective-permute-start.13 = (f32[49,512]{1,0:T(8,128)S(1)}, f32[49,512]{1,0:T(8,128)S(1)}, u32[]{:S(2)}, u32[]{:S(2)}) collective-permute-start(f32[49,512]{1,0:T(8,128)S(1)} %shard_map.79), channel_id=1, source_target_pairs={{0,2},{2,0},{4,6},{6,4},{1,3},{3,1},{5,7},{7,5},{8,10},{10,8},{12,... | collective-permute-start | bytes 301064 | tf_op jit(solution)/shard_map/ppermute | solution.py:271
  130.0 2.8 %copy-start.14 = (f32[2,2,2,16,2048]{4,3,0,1,2:T(8,128)}, f32[2,2,2,16,2048]{4,3,0,1,2:T(8,128)S(1)}, u32[]{:S(2)}) copy-start(f32[2,2,2,16,2048]{4,3,0,1,2:T(8,128)S(1)} %bitcast_add_fusion.1) | copy-start | bytes 3145732
  130.1 8.9 %collective-permute-start.10 = (bf16[2,2,16,2048]{3,2,0,1:T(8,128)(2,1)S(1)}, bf16[2,2,16,2048]{3,2,0,1:T(8,128)(2,1)S(1)}, u32[]{:S(2)}, u32[]{:S(2)}) collective-permute-start(bf16[2,2,16,2048]{3,2,0,1:T(8,128)(2,1)S(1)} %fusion.2), channel_id=1, source_target_pairs={{0,1},{1,0},{2,3},{3,2},{4,5},{5,4},{6,7},{7,6},{8,9},{9,8},{10,11... | collective-permute-start | bytes 786440 | tf_op jit(solution)/shard_map/ppermute | solution.py:271
  132.7 4.5 %collective-permute-start.14 = (f32[49,512]{1,0:T(8,128)S(1)}, f32[49,512]{1,0:T(8,128)S(1)}, u32[]{:S(2)}, u32[]{:S(2)}) collective-permute-start(f32[49,512]{1,0:T(8,128)S(1)} %add.111), channel_id=1, source_target_pairs={{0,4},{2,6},{4,0},{6,2},{1,5},{3,7},{5,1},{7,3},{8,12},{10,14},{12... | collective-permute-start | bytes 301064 | tf_op jit(solution)/shard_map/ppermute | solution.py:271
  132.9 31.0 %copy-start.1 = (bf16[4,8,32,512]{3,2,1,0:T(8,128)(2,1)S(1)}, bf16[4,8,32,512]{3,2,1,0:T(8,128)(2,1)}, u32[]{:S(2)}) copy-start(bf16[4,8,32,512]{3,2,1,0:T(8,128)(2,1)} %rest_0_.1) | copy-start | bytes 3145732
  137.2 7.4 %collective-permute-start.15 = (f32[49,512]{1,0:T(8,128)S(1)}, f32[49,512]{1,0:T(8,128)S(1)}, u32[]{:S(2)}, u32[]{:S(2)}) collective-permute-start(f32[49,512]{1,0:T(8,128)S(1)} %add.112), channel_id=1, source_target_pairs={{0,1},{1,0},{2,3},{3,2},{4,5},{5,4},{6,7},{7,6},{8,9},{9,8},{10,11... | collective-permute-start | bytes 301064 | tf_op jit(solution)/shard_map/ppermute | solution.py:271
  140.1 6.1 %collective-permute-start.11 = (bf16[2,16,2048]{2,1,0:T(8,128)(2,1)S(1)}, bf16[2,16,2048]{2,1,0:T(8,128)(2,1)S(1)}, u32[]{:S(2)}, u32[]{:S(2)}) collective-permute-start(bf16[2,16,2048]{2,1,0:T(8,128)(2,1)S(1)} %fusion.3), channel_id=1, source_target_pairs={{0,8},{8,0},{16,24},{24,16},{1,9},{9,1},{17,25},{25,17},{2,10},{10... | collective-permute-start | bytes 393224 | tf_op jit(solution)/shard_map/ppermute | solution.py:271
  140.3 6.6 %collective-permute-start.4 = (bf16[4,3,32,512]{3,2,1,0:T(8,128)(2,1)S(1)}, bf16[4,3,32,512]{3,2,1,0:T(8,128)(2,1)S(1)}, u32[]{:S(2)}, u32[]{:S(2)}) collective-permute-start(bf16[4,3,32,512]{3,2,1,0:T(8,128)(2,1)S(1)} %get-tuple-element.12), channel_id=1, source_target_pairs={{0,2},{2,4},{4,6},{1,3},{3,5},{5,7},{8,10},{10,12},{12,14},{9,11},... | collective-permute-start | bytes 1179656 | tf_op jit(solution)/shard_map/ppermute | solution.py:22
  142.2 9.4 %collective-permute-start.5 = (bf16[4,3,32,512]{3,2,1,0:T(8,128)(2,1)S(1)}, bf16[4,3,32,512]{3,2,1,0:T(8,128)(2,1)S(1)}, u32[]{:S(2)}, u32[]{:S(2)}) collective-permute-start(bf16[4,3,32,512]{3,2,1,0:T(8,128)(2,1)S(1)} %get-tuple-element.11), channel_id=1, source_target_pairs={{2,0},{4,2},{6,4},{3,1},{5,3},{7,5},{10,8},{12,10},{14,12},{11,9},... | collective-permute-start | bytes 1179656 | tf_op jit(solution)/shard_map/ppermute | solution.py:23
  144.7 12.6 %collective-permute-start.16 = (f32[49,512]{1,0:T(8,128)S(1)}, f32[49,512]{1,0:T(8,128)S(1)}, u32[]{:S(2)}, u32[]{:S(2)}) collective-permute-start(f32[49,512]{1,0:T(8,128)S(1)} %add.113), channel_id=1, source_target_pairs={{0,8},{8,0},{16,24},{24,16},{1,9},{9,1},{17,25},{25,17},{2,10},{10... | collective-permute-start | bytes 301064 | tf_op jit(solution)/shard_map/ppermute | solution.py:271
  146.3 12.6 %collective-permute-start.12 = (bf16[16,2048]{1,0:T(8,128)(2,1)S(1)}, bf16[16,2048]{1,0:T(8,128)(2,1)S(1)}, u32[]{:S(2)}, u32[]{:S(2)}) collective-permute-start(bf16[16,2048]{1,0:T(8,128)(2,1)S(1)} %fusion.5), channel_id=1, source_target_pairs={{0,16},{8,24},{16,0},{24,8},{1,17},{9,25},{17,1},{25,9},{2,18},{10... | collective-permute-start | bytes 196616 | tf_op jit(solution)/shard_map/ppermute | solution.py:271
  151.8 12.0 %collective-permute-start.7 = (bf16[4,14,3,512]{3,2,1,0:T(4,128)(2,1)S(1)}, bf16[4,14,3,512]{3,2,1,0:T(4,128)(2,1)S(1)}, u32[]{:S(2)}, u32[]{:S(2)}) collective-permute-start(bf16[4,14,3,512]{3,2,1,0:T(4,128)(2,1)S(1)} %pad_maximum_fusion.4), channel_id=1, source_target_pairs={{1,0},{3,2},{5,4},{7,6},{9,8},{11,10},{13,12},{15,14},{17,16},{19,... | collective-permute-start | bytes 516104 | tf_op jit(solution)/shard_map/ppermute | solution.py:34
  153.3 10.6 %collective-permute-start.6 = (bf16[4,14,3,512]{3,2,1,0:T(4,128)(2,1)S(1)}, bf16[4,14,3,512]{3,2,1,0:T(4,128)(2,1)S(1)}, u32[]{:S(2)}, u32[]{:S(2)}) collective-permute-start(bf16[4,14,3,512]{3,2,1,0:T(4,128)(2,1)S(1)} %pad_maximum_fusion.3), channel_id=1, source_target_pairs={{0,1},{2,3},{4,5},{6,7},{8,9},{10,11},{12,13},{14,15},{16,17},{18,... | collective-permute-start | bytes 516104 | tf_op jit(solution)/shard_map/ppermute | solution.py:33
  157.4 5.8 %collective-permute-start.17 = (f32[49,512]{1,0:T(8,128)S(1)}, f32[49,512]{1,0:T(8,128)S(1)}, u32[]{:S(2)}, u32[]{:S(2)}) collective-permute-start(f32[49,512]{1,0:T(8,128)S(1)} %add.114), channel_id=1, source_target_pairs={{0,16},{8,24},{16,0},{24,8},{1,17},{9,25},{17,1},{25,9},{2,18},{10... | collective-permute-start | bytes 301064 | tf_op jit(solution)/shard_map/ppermute | solution.py:271
where the time goes:
time: 174 us
  waiting for transfers between devices  67.5 us (39%)
  Pallas kernels  42.8 us (25%)
  starting transfers between devices  42.2 us (24%)
  local copies, waits for them, and re-layouts  13.1 us (8%)
  other arithmetic  6.85 us (4%)
    all_to_all x1, waiting for transfers between devices, on_device(): spread_mixed = lax.all_to_all(mixed, 'frame', 0, 0)  22.1 us
    all_to_all x1, waiting for transfers between devices, on_device(): grad_mixed = lax.all_to_all(token_grad.reshape(mixed.shape), 'frame', 0, 0)  20.8 us
    pallas_call x2, Pallas kernels, conv_call(): pl.pallas_call(functools.partial(conv_kernel, side, half, base is not Non...  19.3 us
    pallas_call x1, Pallas kernels, attend_call(): pl.pallas_call(functools.partial(attend_kernel, heads), grid=(count // ce...  14.7 us
    ppermute x2, waiting for transfers between devices, edges(): high = lax.ppermute(block[:, :width], 'lat', down)  9.29 us
    ppermute x10, waiting for transfers between devices, swapped(): return lax.ppermute(value, axis, [(i, i ^ bit) for i in range(count)])  9.26 us
    pallas_call x1, Pallas kernels, tap_call(): pl.pallas_call(functools.partial(tap_kernel, side, half), grid=(width //...  8.75 us
    ppermute x2, starting transfers between devices, edges(): left = lax.ppermute(strip(cols - width), 'lon', up)  8.02 us
  transfers between devices with their start and end apart: 21, of which 11 were waited for; matrix products, arithmetic and copies ran while one was open for 5% of the time, Pallas kernels for 11%

commit v1 on v0

--- a/solution.py
+++ b/solution.py
@@ -14,13 +14,17 @@
 LIMIT = 40 * 1024 * 1024
 
 
-def edges(block, width):
+def row_edges(block, width):
     count = lax.axis_size("lat")
     up = [(i, i + 1) for i in range(count - 1)]
     down = [(j, i) for i, j in up]
     rows = block.shape[1]
     low = lax.ppermute(block[:, rows - width :], "lat", up)
     high = lax.ppermute(block[:, :width], "lat", down)
+    return low, high
+
+
+def col_edges(block, low, high, width):
     count = lax.axis_size("lon")
     up = [(i, i + 1) for i in range(count - 1)]
     down = [(j, i) for i, j in up]
@@ -32,7 +36,7 @@
 
     left = lax.ppermute(strip(cols - width), "lon", up)
     right = lax.ppermute(strip(0), "lon", down)
-    return low, high, left, right
+    return left, right
 
 
 def fill(scratch, centre, low, high, left, right, half):
@@ -114,7 +118,7 @@
         out[...] = jnp.sum(sums[...], axis=1)
 
 
-def frame_spec(array, lanes, flip):
+def frame_spec(array, lanes, flip, offset=0):
     if array.ndim == 4:
         shape = (1,) + array.shape[1:3] + (lanes,)
         place = lambda f, c: (f, 0, 0, c)
@@ -122,7 +126,7 @@
         shape = (array.shape[0], 1) + array.shape[2:4] + (lanes,)
         place = lambda f, c: (0, f, 0, 0, c)
     if flip:
-        return pl.BlockSpec(shape, lambda c, f: place(f, c))
+        return pl.BlockSpec(shape, lambda c, f: place(f, c + offset))
     return pl.BlockSpec(shape, place)
 
 
@@ -164,18 +168,19 @@
     )(*operands)
 
 
-def tap_call(block, halo, grads, side):
+def tap_call(block, halo, grads, side, part, parts):
     frames, rows, cols, width = block.shape
     lanes = min(LANES, width)
+    blocks = width // lanes // parts
     half = side // 2
     operands = [block, *halo, grads]
-    flops = 2 * frames * rows * cols * width * side * side
+    flops = 2 * frames * rows * cols * width * side * side // parts
     return pl.pallas_call(
         functools.partial(tap_kernel, side, half),
-        grid=(width // lanes, frames),
-        in_specs=[frame_spec(value, lanes, True) for value in operands],
+        grid=(blocks, frames),
+        in_specs=[frame_spec(value, lanes, True, part * blocks) for value in operands],
         out_specs=pl.BlockSpec((side * side, lanes), lambda c, f: (0, c)),
-        out_shape=jax.ShapeDtypeStruct((side * side, width), jnp.float32),
+        out_shape=jax.ShapeDtypeStruct((side * side, blocks * lanes), jnp.float32),
         scratch_shapes=[
             padded_scratch(block, half, lanes),
             pltpu.VMEM((side * side, 8, lanes), jnp.float32),
@@ -280,16 +285,18 @@
     return value
 
 
-def paired_scatter(value, axes, order):
-    sizes = [lax.axis_size(axis) for axis in axes]
+def scatter_digits(axes):
     digits = []
-    for axis, size in zip(axes, sizes):
-        bit = size // 2
+    for axis in axes:
+        bit = lax.axis_size(axis) // 2
         while bit >= 1:
             digits.append((axis, bit))
             bit //= 2
-    rows, cols = value.shape
-    value = value.reshape((2,) * len(digits) + (rows // math.prod(sizes), cols))
+    return digits
+
+
+def paired_scatter(value, digits, order):
+    digits = list(digits)
     for axis in order:
         bit = 1
         while bit < lax.axis_size(axis):
@@ -301,7 +308,7 @@
             came = swapped(away.astype(jnp.bfloat16), axis, bit)
             value = kept.astype(jnp.float32) + came.astype(jnp.float32)
             bit *= 2
-    return value
+    return value, digits
 
 
 def on_device(frames_in, grad_out, kernel, w_qkv, w_out):
@@ -309,7 +316,8 @@
     side = math.isqrt(kernel.shape[0])
     half = side // 2
     parts = lax.axis_size("frame")
-    halo = edges(frames_in, half)
+    halo = row_edges(frames_in, half)
+    halo = halo + col_edges(frames_in, *halo, half)
     share = tile_lat // parts
     grad_parts = grad_out.reshape(local_frames, parts, share, tile_lon, width)
     spread_grad = lax.all_to_all(grad_parts.transpose(1, 0, 2, 3, 4), "frame", 0, 0)
@@ -320,10 +328,23 @@
         spread_mixed.reshape(clip), spread_grad.reshape(clip), w_qkv, w_out, HEADS
     )
     grad_mixed = lax.all_to_all(token_grad.reshape(mixed.shape), "frame", 0, 0)
-    kernel_part = tap_call(frames_in, halo, grad_mixed, side)
+    joined = jnp.concatenate([qkv_part, out_part], axis=1)
+    digits = scatter_digits(("frame", "lat", "lon"))
+    blocks = joined.reshape((2,) * len(digits) + (-1, joined.shape[1]))
+    sums, digits = paired_scatter(blocks, digits, ("lat", "lon"))
+    grad_mixed, sums = lax.optimization_barrier((grad_mixed, sums))
     grad_rows = grad_mixed.transpose(1, 0, 2, 3, 4).reshape(frames_in.shape)
-    grad_halo = edges(grad_rows, half)
-    grad_input = conv_call(grad_mixed, grad_halo, kernel[::-1], grad_out, None)
+    low, high = row_edges(grad_rows, half)
+    first = tap_call(frames_in, halo, grad_mixed, side, 0, 2)
+    low, high, first, sums = lax.optimization_barrier((low, high, first, sums))
+    left, right = col_edges(grad_rows, low, high, half)
+    later_grads, _ = lax.optimization_barrier((grad_mixed, low))
+    second = tap_call(frames_in, halo, later_grads, side, 1, 2)
+    kernel_part = jnp.concatenate([first, second], axis=1)
+    kernel_part, left, right = lax.optimization_barrier((kernel_part, left, right))
+    grad_input = conv_call(
+        grad_mixed, (low, high, left, right), kernel[::-1], grad_out, None
+    )
     total_cells = (
         local_frames
         * lax.axis_size("frame")
@@ -334,8 +355,8 @@
     )
     scale = total_cells ** (-0.5)
     grad_kernel = paired_total(kernel_part, ("lat", "lon", "frame")) * scale
-    joined = jnp.concatenate([qkv_part, out_part], axis=1)
-    grad_proj = paired_scatter(joined, ("frame", "lat", "lon"), ("lat", "lon", "frame")) * scale
+    sums, digits = paired_scatter(sums, digits, ("frame",))
+    grad_proj = sums * scale
     return (grad_input, grad_proj, grad_kernel)
 
 

time: 174 us -> 192 us (1.10)
  the two profiles are of different devices: /device:TPU:1 before, /device:TPU:0 now
where the time goes in v1:
time: 192 us; the launch traced here: 190 us
  waiting for transfers between devices  68.3 us (36%)
  Pallas kernels  44.9 us (23%)
  starting transfers between devices  44.6 us (23%)
  local copies, waits for them, and re-layouts  19.6 us (10%)
  other arithmetic  11.5 us (6%)
    ppermute x10, waiting for transfers between devices, swapped(): return lax.ppermute(value, axis, [(i, i ^ bit) for i in range(count)])  31.8 us
    all_to_all x1, waiting for transfers between devices, on_device(): spread_mixed = lax.all_to_all(mixed, 'frame', 0, 0)  26.1 us
    pallas_call x2, Pallas kernels, conv_call(): pl.pallas_call(functools.partial(conv_kernel, side, half, base is not Non...  20.7 us
    pallas_call x1, Pallas kernels, attend_call(): pl.pallas_call(functools.partial(attend_kernel, heads), grid=(count // ce...  15.5 us
    ppermute x10, starting transfers between devices, swapped(): return lax.ppermute(value, axis, [(i, i ^ bit) for i in range(count)])  14.2 us
    unnamed x50, local copies, waits for them, and re-layouts  12.4 us
    pallas_call x2, Pallas kernels, tap_call(): pl.pallas_call(functools.partial(tap_kernel, side, half), grid=(blocks, f...  8.79 us
    all_to_all x1, starting transfers between devices, on_device(): lax.all_to_all(grad_parts.transpose(1, 0, 2, 3, 4), 'frame', 0, 0)  6.45 us
  transfers between devices with their start and end apart: 21, of which 11 were waited for; matrix products, arithmetic and copies ran while one was open for 6% of the time, Pallas kernels for 15%

profile of v1, /device:TPU:0, one launch (start us, length us, event | category | flops | bytes accessed | tf_op | source)
XLA Modules:
  0.0 190.1 jit_solution(5804065105150216882)
XLA Ops:
  0.6 2.4 %copy.18 = bf16[4,4,2,32,512]{4,3,2,0,1:T(8,128)(2,1)} copy(bf16[4,4,2,32,512]{4,3,2,1,0:T(8,128)(2,1)} %bitcast.33) | data formatting | bytes 2097152 | tf_op jit(solution)/shard_map/reshape | solution.py:322
  3.1 6.4 %all-to-all-start.1 = ((bf16[4,4,2,32,512]{4,3,2,1,0:T(8,128)(2,1)}), bf16[4,4,2,32,512]{4,3,2,1,0:T(8,128)(2,1)S(1)}, u32[]{:S(2)}, u32[]{:S(2)}) async-start(bf16[4,4,2,32,512]{4,3,2,1,0:T(8,128)(2,1)} %bitcast.31), calls=%async_computation.1 | async-start | bytes 2097152 | tf_op jit(solution)/shard_map/all_to_all | solution.py:323
  9.6 1.3 collective-permute-start.1
  10.9 3.1 %collective-permute-start = (bf16[4,3,32,512]{3,2,1,0:T(8,128)(2,1)S(1)}, bf16[4,3,32,512]{3,2,1,0:T(8,128)(2,1)S(1)}, u32[]{:S(2)}, u32[]{:S(2)}) collective-permute-start(bf16[4,3,32,512]{3,2,1,0:T(8,128)(2,1)S(1)} %get-tuple-element.36), channel_id=1, source_target_pairs={{0,2},{2,4},{4,6},{1,3},{3,5},{5,7},{8,10},{10,12},{12,14},{9,11},... | collective-permute-start | bytes 1179656 | tf_op jit(solution)/shard_map/ppermute | solution.py:22
  14.1 1.1 collective-permute-done.low
  15.5 3.4 %collective-permute-start.2 = (bf16[4,14,3,512]{3,2,1,0:T(4,128)(2,1)S(1)}, bf16[4,14,3,512]{3,2,1,0:T(4,128)(2,1)S(1)}, u32[]{:S(2)}, u32[]{:S(2)}) collective-permute-start(bf16[4,14,3,512]{3,2,1,0:T(4,128)(2,1)S(1)} %pad_maximum_fusion.1), channel_id=1, source_target_pairs={{0,1},{2,3},{4,5},{6,7},{8,9},{10,11},{12,13},{14,15},{16,17},{18,... | collective-permute-start | bytes 516104 | tf_op jit(solution)/shard_map/ppermute | solution.py:37
  19.1 1.3 collective-permute-start.3
  20.4 2.0 %collective-permute-done.2.left = bf16[4,14,3,512]{3,2,1,0:T(4,128)(2,1)S(1)} collective-permute-done((bf16[4,14,3,512]{3,2,1,0:T(4,128)(2,1)S(1)}, bf16[4,14,3,512]{3,2,1,0:T(4,128)(2,1)S(1)}, u32[]{:S(2)}, u32[]{:S(2)}) %collective-permute-start.2) | collective-permute-done | bytes 172064 | tf_op jit(solution)/shard_map/ppermute | solution.py:37
  22.4 4.6 %collective-permute-done.3.right = bf16[4,14,3,512]{3,2,1,0:T(4,128)(2,1)S(1)} collective-permute-done((bf16[4,14,3,512]{3,2,1,0:T(4,128)(2,1)S(1)}, bf16[4,14,3,512]{3,2,1,0:T(4,128)(2,1)S(1)}, u32[]{:S(2)}, u32[]{:S(2)}) %collective-permute-start.3) | collective-permute-done | bytes 172064 | tf_op jit(solution)/shard_map/ppermute | solution.py:38
  27.0 9.6 %shard_map.76 = bf16[4,4,2,32,512]{4,3,2,1,0:T(8,128)(2,1)} custom-call(bf16[4,8,32,512]{3,2,1,0:T(8,128)(2,1)S(1)} %copy-done, bf16[4,3,32,512]{3,2,1,0:T(8,128)(2,1)S(1)} %collective-permute-done.low, bf16[4,3,32,512]{3,2,1,0:T(8,128)(2,1)S(1)} %collective-permute-done.1.high, bf16[4,14,3,512]{3,2,1,0:T(4,128)(2,1)S(1)} %collective-permute-done.2.left, ...), custom_call_target="tpu_custom_call" | custom-call | flops 51380224 | bytes 2097152 | tf_op jit(solution)/shard_map/pallas_call | solution.py:159
  37.3 5.1 %all-to-all-start = ((bf16[4,4,2,32,512]{4,3,2,1,0:T(8,128)(2,1)}), bf16[4,4,2,32,512]{4,3,2,1,0:T(8,128)(2,1)S(1)}, u32[]{:S(2)}, u32[]{:S(2)}) async-start(bf16[4,4,2,32,512]{4,3,2,1,0:T(8,128)(2,1)} %shard_map.76), calls=%async_computation | async-start | bytes 2097152 | tf_op jit(solution)/shard_map/all_to_all | solution.py:325
  42.4 26.1 %all-to-all-done = bf16[4,4,2,32,512]{4,3,2,1,0:T(8,128)(2,1)S(1)} async-done(((bf16[4,4,2,32,512]{4,3,2,1,0:T(8,128)(2,1)}), bf16[4,4,2,32,512]{4,3,2,1,0:T(8,128)(2,1)S(1)}, u32[]{:S(2)}, u32[]{:S(2)}) %all-to-all-start) | async-done | bytes 1048608 | tf_op jit(solution)/shard_map/all_to_all | solution.py:325
  68.4 1.4 copy-done.11
  69.9 1.0 copy-done.16
  70.9 15.5 %shard_map.77 = (bf16[16,64,512]{2,1,0:T(8,128)(2,1)}, f32[512,1536]{1,0:T(8,128)S(1)}, f32[512,512]{1,0:T(8,128)S(1)}) custom-call(bf16[16,64,512]{2,1,0:T(8,128)(2,1)S(1)} %bitcast.35, bf16[16,64,512]{2,1,0:T(8,128)(2,1)S(1)} %bitcast.34, bf16[512,1536]{1,0:T(8,128)(2,1)S(1)} %copy-done.11, bf16[512,512]{1,0:T(8,128)(2,1)S(1)} %copy-done.16), custom_call_target="tpu_custom_call" | custom-call | tf_op jit(solution)/shard_map/pallas_call | solution.py:256
  86.6 2.0 %copy-done.19 = f32[512,2048]{1,0:T(8,128)} copy-done((f32[512,2048]{1,0:T(8,128)}, f32[512,2048]{1,0:T(8,128)S(1)}, u32[]{:S(2)}) %copy-start.19) | copy-done | bytes 4194328
  88.8 1.0 collective-permute-start.4
  89.7 2.3 %collective-permute-done.4 = bf16[2,2,2,2,16,2048]{5,4,0,1,3,2:T(8,128)(2,1)S(1)} collective-permute-done((bf16[2,2,2,2,16,2048]{5,4,0,1,3,2:T(8,128)(2,1)S(1)}, bf16[2,2,2,2,16,2048]{5,4,0,1,3,2:T(8,128)(2,1)S(1)}, u32[]{:S(2)}, u32[]{:S(2)}) %collective-permute-start.4) | collective-permute-done | bytes 1048608 | tf_op jit(solution)/shard_map/ppermute | solution.py:276
  92.0 1.8 bitcast_add_fusion
  93.9 1.3 copy-done.20
  95.3 3.5 %all-to-all-start.2 = ((bf16[4,4,2,32,512]{4,3,2,1,0:T(8,128)(2,1)}), bf16[4,4,2,32,512]{4,3,2,1,0:T(8,128)(2,1)S(1)}, u32[]{:S(2)}, u32[]{:S(2)}) async-start(bf16[4,4,2,32,512]{4,3,2,1,0:T(8,128)(2,1)} %bitcast.4), calls=%async_computation.2 | async-start | bytes 2097152 | tf_op jit(solution)/shard_map/all_to_all | solution.py:330
  98.9 10.6 %collective-permute-done.5 = bf16[2,2,2,16,2048]{4,3,0,1,2:T(8,128)(2,1)S(1)} collective-permute-done((bf16[2,2,2,16,2048]{4,3,0,1,2:T(8,128)(2,1)S(1)}, bf16[2,2,2,16,2048]{4,3,0,1,2:T(8,128)(2,1)S(1)}, u32[]{:S(2)}, u32[]{:S(2)}) %collective-permute-start.5) | collective-permute-done | bytes 524320 | tf_op jit(solution)/shard_map/ppermute | solution.py:276
  109.5 1.3 bitcast_add_fusion.1
  110.9 1.0 copy-done.21
  112.6 8.1 %collective-permute-done.6 = bf16[2,2,16,2048]{3,2,0,1:T(8,128)(2,1)} collective-permute-done((bf16[2,2,16,2048]{3,2,0,1:T(8,128)(2,1)}, bf16[2,2,16,2048]{3,2,0,1:T(8,128)(2,1)}, u32[]{:S(2)}, u32[]{:S(2)}) %collective-permute-start.6) | collective-permute-done | bytes 262176 | tf_op jit(solution)/shard_map/ppermute | solution.py:276
  120.7 2.0 %bitcast_add_fusion.2 = f32[2,2,16,2048]{3,2,0,1:T(8,128)} fusion(bf16[2,2,16,2048]{3,2,0,1:T(8,128)(2,1)} %collective-permute-done.6, f32[2,2,2,16,2048]{4,3,0,1,2:T(8,128)} %copy-done.21, s32[]{:T(128)S(6)} %select_n.76), kind=kLoop, calls=%fused_computation.8 | loop fusion | flops 262144 | bytes 1310724 | tf_op jit(solution)/shard_map/add | solution.py:309
  122.7 2.7 %all-to-all-done.2.grads.centre = bf16[4,4,2,32,512]{4,3,2,1,0:T(8,128)(2,1)S(1)} async-done(((bf16[4,4,2,32,512]{4,3,2,1,0:T(8,128)(2,1)}), bf16[4,4,2,32,512]{4,3,2,1,0:T(8,128)(2,1)S(1)}, u32[]{:S(2)}, u32[]{:S(2)}) %all-to-all-start.2) | async-done | bytes 1048608 | tf_op jit(solution)/shard_map/all_to_all | solution.py:330
  125.6 1.5 collective-permute-start.7
  127.1 1.3 collective-permute-start.8
  128.4 4.4 %shard_map.78 = f32[49,256]{1,0:T(8,128)S(1)} custom-call(bf16[4,8,32,512]{3,2,1,0:T(8,128)(2,1)S(1)} %copy-done, bf16[4,3,32,512]{3,2,1,0:T(8,128)(2,1)S(1)} %copy-done.3, bf16[4,3,32,512]{3,2,1,0:T(8,128)(2,1)S(1)} %collective-permute-done.1.high, bf16[4,14,3,512]{3,2,1,0:T(4,128)(2,1)S(1)} %copy-done.6, bf16[4,14,3,512]{3,2,1,0:T(4,128)(2,1)S(1)} %copy-done.9, ...), custom_call_target="tpu_custom_call" | custom-call | flops 25690112 | bytes 2097152 | tf_op jit(solution)/shard_map/pallas_call | solution.py:178
  134.0 2.1 %collective-permute-start.9 = (bf16[4,14,3,512]{3,2,1,0:T(4,128)(2,1)}, bf16[4,14,3,512]{3,2,1,0:T(4,128)(2,1)}, u32[]{:S(2)}, u32[]{:S(2)}) collective-permute-start(bf16[4,14,3,512]{3,2,1,0:T(4,128)(2,1)} %pad_maximum_fusion.3), channel_id=1, source_target_pairs={{0,1},{2,3},{4,5},{6,7},{8,9},{10,11},{12,13},{14,15},{16,17},{18,... | collective-permute-start | bytes 516104 | tf_op jit(solution)/shard_map/ppermute | solution.py:37
  136.9 1.4 collective-permute-start.10
  138.4 1.0 copy-done.4
  141.3 4.4 %shard_map.79 = f32[49,256]{1,0:T(8,128)S(1)} custom-call(bf16[4,8,32,512]{3,2,1,0:T(8,128)(2,1)S(1)} %copy-done, bf16[4,3,32,512]{3,2,1,0:T(8,128)(2,1)S(1)} %copy-done.4, bf16[4,3,32,512]{3,2,1,0:T(8,128)(2,1)S(1)} %collective-permute-done.1.high, bf16[4,14,3,512]{3,2,1,0:T(4,128)(2,1)S(1)} %copy-done.7, bf16[4,14,3,512]{3,2,1,0:T(4,128)(2,1)S(1)} %copy-done.10, ...), custom_call_target="tpu_custom_call" | custom-call | flops 25690112 | bytes 2097152 | tf_op jit(solution)/shard_map/pallas_call | solution.py:178
  145.7 5.4 %collective-permute-start.13 = (f32[49,512]{1,0:T(8,128)S(1)}, f32[49,512]{1,0:T(8,128)S(1)}, u32[]{:S(2)}, u32[]{:S(2)}) collective-permute-start(f32[49,512]{1,0:T(8,128)S(1)} %pad_maximum_fusion.5), channel_id=1, source_target_pairs={{0,2},{2,0},{4,6},{6,4},{1,3},{3,1},{5,7},{7,5},{8,10},{10,8},{12,... | collective-permute-start | bytes 301064 | tf_op jit(solution)/shard_map/ppermute | solution.py:276
  151.1 1.0 fusion.3
  152.4 5.2 %collective-permute-done.14 = f32[49,512]{1,0:T(8,128)S(1)} collective-permute-done((f32[49,512]{1,0:T(8,128)S(1)}, f32[49,512]{1,0:T(8,128)S(1)}, u32[]{:S(2)}, u32[]{:S(2)}) %collective-permute-start.14) | collective-permute-done | bytes 100384 | tf_op jit(solution)/shard_map/ppermute | solution.py:276
  157.5 3.1 %collective-permute-start.15 = (f32[49,512]{1,0:T(8,128)S(1)}, f32[49,512]{1,0:T(8,128)S(1)}, u32[]{:S(2)}, u32[]{:S(2)}) collective-permute-start(f32[49,512]{1,0:T(8,128)S(1)} %add.112), channel_id=1, source_target_pairs={{0,1},{1,0},{2,3},{3,2},{4,5},{5,4},{6,7},{7,6},{8,9},{9,8},{10,11... | collective-permute-start | bytes 301064 | tf_op jit(solution)/shard_map/ppermute | solution.py:276
  160.7 1.0 bitcast_add_fusion.3
  161.6 1.8 collective-permute-done.15
  164.1 1.5 collective-permute-start.16
  166.7 1.5 rev.3
  168.4 1.0 copy-done.13
  169.4 1.0 copy-done.15
  170.4 11.1 %shard_map.80 = bf16[4,8,32,512]{3,2,1,0:T(8,128)(2,1)} custom-call(bf16[4,4,2,32,512]{4,3,2,1,0:T(8,128)(2,1)S(1)} %all-to-all-done.2.grads.centre, bf16[4,3,32,512]{3,2,1,0:T(8,128)(2,1)S(1)} %copy-done.13, bf16[4,3,32,512]{3,2,1,0:T(8,128)(2,1)S(1)} %copy-done.15, bf16[4,14,3,512]{3,2,1,0:T(4,128)(2,1)} %collective-permute-done.9.left, ...), custom_call_target="tpu_custom_call" | custom-call | flops 51380224 | bytes 2097152 | tf_op jit(solution)/shard_map/pallas_call | solution.py:159
  181.5 1.0 add.114
  182.5 2.4 %collective-permute-start.17 = (f32[49,512]{1,0:T(8,128)S(1)}, f32[49,512]{1,0:T(8,128)S(1)}, u32[]{:S(2)}, u32[]{:S(2)}) collective-permute-start(f32[49,512]{1,0:T(8,128)S(1)} %add.114), channel_id=1, source_target_pairs={{0,16},{8,24},{16,0},{24,8},{1,17},{9,25},{17,1},{25,9},{2,18},{10... | collective-permute-start | bytes 301064 | tf_op jit(solution)/shard_map/ppermute | solution.py:276
  185.6 3.9 %collective-permute-done.17 = f32[49,512]{1,0:T(8,128)S(1)} collective-permute-done((f32[49,512]{1,0:T(8,128)S(1)}, f32[49,512]{1,0:T(8,128)S(1)}, u32[]{:S(2)}, u32[]{:S(2)}) %collective-permute-start.17) | collective-permute-done | bytes 100384 | tf_op jit(solution)/shard_map/ppermute | solution.py:276
  (82 shorter events, 10.3 us)
Async XLA Ops:
  0.6 8.9 %copy-start = (bf16[4,8,32,512]{3,2,1,0:T(8,128)(2,1)S(1)}, bf16[4,8,32,512]{3,2,1,0:T(8,128)(2,1)}, u32[]{:S(2)}) copy-start(bf16[4,8,32,512]{3,2,1,0:T(8,128)(2,1)} %centre.5) | copy-start | bytes 3145732
  3.1 17.3 %copy-start.24 = (bf16[49,512]{1,0:T(8,128)(2,1)S(1)}, bf16[49,512]{1,0:T(8,128)(2,1)}, u32[]{:S(2)}) copy-start(bf16[49,512]{1,0:T(8,128)(2,1)} %param.7) | copy-start | bytes 150532
  3.1 34.2 %all-to-all-start.1 = ((bf16[4,4,2,32,512]{4,3,2,1,0:T(8,128)(2,1)}), bf16[4,4,2,32,512]{4,3,2,1,0:T(8,128)(2,1)S(1)}, u32[]{:S(2)}, u32[]{:S(2)}) async-start(bf16[4,4,2,32,512]{4,3,2,1,0:T(8,128)(2,1)} %bitcast.31), calls=%async_computation.1 | async-start | bytes 2097152 | tf_op jit(solution)/shard_map/all_to_all | solution.py:323
  9.6 4.5 %collective-permute-start.1 = (bf16[4,3,32,512]{3,2,1,0:T(8,128)(2,1)S(1)}, bf16[4,3,32,512]{3,2,1,0:T(8,128)(2,1)S(1)}, u32[]{:S(2)}, u32[]{:S(2)}) collective-permute-start(bf16[4,3,32,512]{3,2,1,0:T(8,128)(2,1)S(1)} %get-tuple-element.35), channel_id=1, source_target_pairs={{2,0},{4,2},{6,4},{3,1},{5,3},{7,5},{10,8},{12,10},{14,12},{11,9},... | collective-permute-start | bytes 1179656 | tf_op jit(solution)/shard_map/ppermute | solution.py:23
  10.9 4.4 %collective-permute-start = (bf16[4,3,32,512]{3,2,1,0:T(8,128)(2,1)S(1)}, bf16[4,3,32,512]{3,2,1,0:T(8,128)(2,1)S(1)}, u32[]{:S(2)}, u32[]{:S(2)}) collective-permute-start(bf16[4,3,32,512]{3,2,1,0:T(8,128)(2,1)S(1)} %get-tuple-element.36), channel_id=1, source_target_pairs={{0,2},{2,4},{4,6},{1,3},{3,5},{5,7},{8,10},{10,12},{12,14},{9,11},... | collective-permute-start | bytes 1179656 | tf_op jit(solution)/shard_map/ppermute | solution.py:22
  15.3 11.7 %copy-start.2 = (bf16[4,3,32,512]{3,2,1,0:T(8,128)(2,1)}, bf16[4,3,32,512]{3,2,1,0:T(8,128)(2,1)S(1)}, u32[]{:S(2)}) copy-start(bf16[4,3,32,512]{3,2,1,0:T(8,128)(2,1)S(1)} %collective-permute-done.low) | copy-start | bytes 1179652
  15.5 6.9 %collective-permute-start.2 = (bf16[4,14,3,512]{3,2,1,0:T(4,128)(2,1)S(1)}, bf16[4,14,3,512]{3,2,1,0:T(4,128)(2,1)S(1)}, u32[]{:S(2)}, u32[]{:S(2)}) collective-permute-start(bf16[4,14,3,512]{3,2,1,0:T(4,128)(2,1)S(1)} %pad_maximum_fusion.1), channel_id=1, source_target_pairs={{0,1},{2,3},{4,5},{6,7},{8,9},{10,11},{12,13},{14,15},{16,17},{18,... | collective-permute-start | bytes 516104 | tf_op jit(solution)/shard_map/ppermute | solution.py:37
  19.1 7.9 %collective-permute-start.3 = (bf16[4,14,3,512]{3,2,1,0:T(4,128)(2,1)S(1)}, bf16[4,14,3,512]{3,2,1,0:T(4,128)(2,1)S(1)}, u32[]{:S(2)}, u32[]{:S(2)}) collective-permute-start(bf16[4,14,3,512]{3,2,1,0:T(4,128)(2,1)S(1)} %pad_maximum_fusion.2), channel_id=1, source_target_pairs={{1,0},{3,2},{5,4},{7,6},{9,8},{11,10},{13,12},{15,14},{17,16},{19,... | collective-permute-start | bytes 516104 | tf_op jit(solution)/shard_map/ppermute | solution.py:38
  22.4 14.9 %copy-start.5 = (bf16[4,14,3,512]{3,2,1,0:T(4,128)(2,1)}, bf16[4,14,3,512]{3,2,1,0:T(4,128)(2,1)S(1)}, u32[]{:S(2)}) copy-start(bf16[4,14,3,512]{3,2,1,0:T(4,128)(2,1)S(1)} %collective-permute-done.2.left) | copy-start | bytes 516100
  36.6 0.7 copy-start.8
  37.3 31.2 %all-to-all-start = ((bf16[4,4,2,32,512]{4,3,2,1,0:T(8,128)(2,1)}), bf16[4,4,2,32,512]{4,3,2,1,0:T(8,128)(2,1)S(1)}, u32[]{:S(2)}, u32[]{:S(2)}) async-start(bf16[4,4,2,32,512]{4,3,2,1,0:T(8,128)(2,1)} %shard_map.76), calls=%async_computation | async-start | bytes 2097152 | tf_op jit(solution)/shard_map/all_to_all | solution.py:325
  68.4 1.4 copy-start.11
  69.8 1.0 copy-start.16
  86.6 2.0 %copy-start.19 = (f32[512,2048]{1,0:T(8,128)}, f32[512,2048]{1,0:T(8,128)S(1)}, u32[]{:S(2)}) copy-start(f32[512,2048]{1,0:T(8,128)S(1)} %pad_maximum_fusion) | copy-start | bytes 12582916
  88.8 3.2 %collective-permute-start.4 = (bf16[2,2,2,2,16,2048]{5,4,0,1,3,2:T(8,128)(2,1)S(1)}, bf16[2,2,2,2,16,2048]{5,4,0,1,3,2:T(8,128)(2,1)S(1)}, u32[]{:S(2)}, u32[]{:S(2)}) collective-permute-start(bf16[2,2,2,2,16,2048]{5,4,0,1,3,2:T(8,128)(2,1)S(1)} %fusion), channel_id=1, source_target_pairs={{0,2},{2,0},{4,6},{6,4},{1,3},{3,1},{5,7},{7,5},{8,10},{10,8},{12,... | collective-permute-start | bytes 3145736 | tf_op jit(solution)/shard_map/ppermute | solution.py:276
  93.8 1.4 copy-start.20
  95.3 14.3 %collective-permute-start.5 = (bf16[2,2,2,16,2048]{4,3,0,1,2:T(8,128)(2,1)S(1)}, bf16[2,2,2,16,2048]{4,3,0,1,2:T(8,128)(2,1)S(1)}, u32[]{:S(2)}, u32[]{:S(2)}) collective-permute-start(bf16[2,2,2,16,2048]{4,3,0,1,2:T(8,128)(2,1)S(1)} %fusion.1), channel_id=1, source_target_pairs={{0,4},{2,6},{4,0},{6,2},{1,5},{3,7},{5,1},{7,3},{8,12},{10,14},{12... | collective-permute-start | bytes 1572872 | tf_op jit(solution)/shard_map/ppermute | solution.py:276
  95.3 30.0 %all-to-all-start.2 = ((bf16[4,4,2,32,512]{4,3,2,1,0:T(8,128)(2,1)}), bf16[4,4,2,32,512]{4,3,2,1,0:T(8,128)(2,1)S(1)}, u32[]{:S(2)}, u32[]{:S(2)}) async-start(bf16[4,4,2,32,512]{4,3,2,1,0:T(8,128)(2,1)} %bitcast.4), calls=%async_computation.2 | async-start | bytes 2097152 | tf_op jit(solution)/shard_map/all_to_all | solution.py:330
  110.9 1.0 copy-start.21
  111.9 16.5 %copy-start.3 = (bf16[4,3,32,512]{3,2,1,0:T(8,128)(2,1)S(1)}, bf16[4,3,32,512]{3,2,1,0:T(8,128)(2,1)}, u32[]{:S(2)}) copy-start(bf16[4,3,32,512]{3,2,1,0:T(8,128)(2,1)} %copy-done.2) | copy-start | bytes 1179652
  111.9 16.5 %copy-start.6 = (bf16[4,14,3,512]{3,2,1,0:T(4,128)(2,1)S(1)}, bf16[4,14,3,512]{3,2,1,0:T(4,128)(2,1)}, u32[]{:S(2)}) copy-start(bf16[4,14,3,512]{3,2,1,0:T(4,128)(2,1)} %copy-done.5) | copy-start | bytes 516100
  111.9 16.5 %copy-start.9 = (bf16[4,14,3,512]{3,2,1,0:T(4,128)(2,1)S(1)}, bf16[4,14,3,512]{3,2,1,0:T(4,128)(2,1)}, u32[]{:S(2)}) copy-start(bf16[4,14,3,512]{3,2,1,0:T(4,128)(2,1)} %copy-done.8) | copy-start | bytes 516100
  112.6 8.1 %collective-permute-start.6 = (bf16[2,2,16,2048]{3,2,0,1:T(8,128)(2,1)}, bf16[2,2,16,2048]{3,2,0,1:T(8,128)(2,1)}, u32[]{:S(2)}, u32[]{:S(2)}) collective-permute-start(bf16[2,2,16,2048]{3,2,0,1:T(8,128)(2,1)} %fusion.2), channel_id=1, source_target_pairs={{0,1},{1,0},{2,3},{3,2},{4,5},{5,4},{6,7},{7,6},{8,9},{9,8},{10,11... | collective-permute-start | bytes 786440 | tf_op jit(solution)/shard_map/ppermute | solution.py:276
  125.6 7.4 %collective-permute-start.7 = (bf16[4,3,32,512]{3,2,1,0:T(8,128)(2,1)S(1)}, bf16[4,3,32,512]{3,2,1,0:T(8,128)(2,1)S(1)}, u32[]{:S(2)}, u32[]{:S(2)}) collective-permute-start(bf16[4,3,32,512]{3,2,1,0:T(8,128)(2,1)S(1)} %get-tuple-element.32), channel_id=1, source_target_pairs={{0,2},{2,4},{4,6},{1,3},{3,5},{5,7},{8,10},{10,12},{12,14},{9,11},... | collective-permute-start | bytes 1179656 | tf_op jit(solution)/shard_map/ppermute | solution.py:22
  127.1 5.9 %collective-permute-start.8 = (bf16[4,3,32,512]{3,2,1,0:T(8,128)(2,1)S(1)}, bf16[4,3,32,512]{3,2,1,0:T(8,128)(2,1)S(1)}, u32[]{:S(2)}, u32[]{:S(2)}) collective-permute-start(bf16[4,3,32,512]{3,2,1,0:T(8,128)(2,1)S(1)} %get-tuple-element.31), channel_id=1, source_target_pairs={{2,0},{4,2},{6,4},{3,1},{5,3},{7,5},{10,8},{12,10},{14,12},{11,9},... | collective-permute-start | bytes 1179656 | tf_op jit(solution)/shard_map/ppermute | solution.py:23
  132.8 3.3 %copy-start.17 = (f32[49,256]{1,0:T(8,128)}, f32[49,256]{1,0:T(8,128)S(1)}, u32[]{:S(2)}) copy-start(f32[49,256]{1,0:T(8,128)S(1)} %shard_map.78) | copy-start | bytes 150532
  133.0 3.1 %copy-start.12 = (bf16[4,3,32,512]{3,2,1,0:T(8,128)(2,1)}, bf16[4,3,32,512]{3,2,1,0:T(8,128)(2,1)S(1)}, u32[]{:S(2)}) copy-start(bf16[4,3,32,512]{3,2,1,0:T(8,128)(2,1)S(1)} %collective-permute-done.7.low) | copy-start | bytes 1179652
  133.0 4.0 %copy-start.14 = (bf16[4,3,32,512]{3,2,1,0:T(8,128)(2,1)}, bf16[4,3,32,512]{3,2,1,0:T(8,128)(2,1)S(1)}, u32[]{:S(2)}) copy-start(bf16[4,3,32,512]{3,2,1,0:T(8,128)(2,1)S(1)} %collective-permute-done.8.high) | copy-start | bytes 1179652
  134.0 11.7 %collective-permute-start.9 = (bf16[4,14,3,512]{3,2,1,0:T(4,128)(2,1)}, bf16[4,14,3,512]{3,2,1,0:T(4,128)(2,1)}, u32[]{:S(2)}, u32[]{:S(2)}) collective-permute-start(bf16[4,14,3,512]{3,2,1,0:T(4,128)(2,1)} %pad_maximum_fusion.3), channel_id=1, source_target_pairs={{0,1},{2,3},{4,5},{6,7},{8,9},{10,11},{12,13},{14,15},{16,17},{18,... | collective-permute-start | bytes 516104 | tf_op jit(solution)/shard_map/ppermute | solution.py:37
  136.9 31.4 %copy-start.1 = (bf16[4,8,32,512]{3,2,1,0:T(8,128)(2,1)S(1)}, bf16[4,8,32,512]{3,2,1,0:T(8,128)(2,1)}, u32[]{:S(2)}) copy-start(bf16[4,8,32,512]{3,2,1,0:T(8,128)(2,1)} %rest_0_.1) | copy-start | bytes 3145732
  136.9 8.8 %collective-permute-start.10 = (bf16[4,14,3,512]{3,2,1,0:T(4,128)(2,1)}, bf16[4,14,3,512]{3,2,1,0:T(4,128)(2,1)}, u32[]{:S(2)}, u32[]{:S(2)}) collective-permute-start(bf16[4,14,3,512]{3,2,1,0:T(4,128)(2,1)} %pad_maximum_fusion.4), channel_id=1, source_target_pairs={{1,0},{3,2},{5,4},{7,6},{9,8},{11,10},{13,12},{15,14},{17,16},{19,... | collective-permute-start | bytes 516104 | tf_op jit(solution)/shard_map/ppermute | solution.py:38
  138.4 1.0 copy-start.4
  139.4 0.9 copy-start.7
  140.3 0.9 copy-start.10
  141.3 4.4 %copy-start.18 = (f32[49,256]{1,0:T(8,128)S(1)}, f32[49,256]{1,0:T(8,128)}, u32[]{:S(2)}) copy-start(f32[49,256]{1,0:T(8,128)} %copy-done.17) | copy-start | bytes 150532
  145.7 6.4 %collective-permute-start.13 = (f32[49,512]{1,0:T(8,128)S(1)}, f32[49,512]{1,0:T(8,128)S(1)}, u32[]{:S(2)}, u32[]{:S(2)}) collective-permute-start(f32[49,512]{1,0:T(8,128)S(1)} %pad_maximum_fusion.5), channel_id=1, source_target_pairs={{0,2},{2,0},{4,6},{6,4},{1,3},{3,1},{5,7},{7,5},{8,10},{10,8},{12,... | collective-permute-start | bytes 301064 | tf_op jit(solution)/shard_map/ppermute | solution.py:276
  152.0 8.6 %collective-permute-start.11 = (bf16[2,16,2048]{2,1,0:T(8,128)(2,1)S(1)}, bf16[2,16,2048]{2,1,0:T(8,128)(2,1)S(1)}, u32[]{:S(2)}, u32[]{:S(2)}) collective-permute-start(bf16[2,16,2048]{2,1,0:T(8,128)(2,1)S(1)} %fusion.3), channel_id=1, source_target_pairs={{0,8},{8,0},{16,24},{24,16},{1,9},{9,1},{17,25},{25,17},{2,10},{10... | collective-permute-start | bytes 393224 | tf_op jit(solution)/shard_map/ppermute | solution.py:276
  152.1 5.4 %collective-permute-start.14 = (f32[49,512]{1,0:T(8,128)S(1)}, f32[49,512]{1,0:T(8,128)S(1)}, u32[]{:S(2)}, u32[]{:S(2)}) collective-permute-start(f32[49,512]{1,0:T(8,128)S(1)} %add.111), channel_id=1, source_target_pairs={{0,4},{2,6},{4,0},{6,2},{1,5},{3,7},{5,1},{7,3},{8,12},{10,14},{12... | collective-permute-start | bytes 301064 | tf_op jit(solution)/shard_map/ppermute | solution.py:276
  157.5 5.9 %collective-permute-start.15 = (f32[49,512]{1,0:T(8,128)S(1)}, f32[49,512]{1,0:T(8,128)S(1)}, u32[]{:S(2)}, u32[]{:S(2)}) collective-permute-start(f32[49,512]{1,0:T(8,128)S(1)} %add.112), channel_id=1, source_target_pairs={{0,1},{1,0},{2,3},{3,2},{4,5},{5,4},{6,7},{7,6},{8,9},{9,8},{10,11... | collective-permute-start | bytes 301064 | tf_op jit(solution)/shard_map/ppermute | solution.py:276
  161.6 6.7 %copy-start.22 = (f32[2,16,2048]{2,1,0:T(8,128)}, f32[2,16,2048]{2,1,0:T(8,128)S(1)}, u32[]{:S(2)}) copy-start(f32[2,16,2048]{2,1,0:T(8,128)S(1)} %bitcast_add_fusion.3) | copy-start | bytes 786436
  164.1 17.4 %collective-permute-start.16 = (f32[49,512]{1,0:T(8,128)}, f32[49,512]{1,0:T(8,128)}, u32[]{:S(2)}, u32[]{:S(2)}) collective-permute-start(f32[49,512]{1,0:T(8,128)} %add.113), channel_id=1, source_target_pairs={{0,8},{8,0},{16,24},{24,16},{1,9},{9,1},{17,25},{25,17},{2,10},{10... | collective-permute-start | bytes 301064 | tf_op jit(solution)/shard_map/ppermute | solution.py:276
  166.2 18.7 %collective-permute-start.12 = (bf16[16,2048]{1,0:T(8,128)(2,1)}, bf16[16,2048]{1,0:T(8,128)(2,1)S(1)}, u32[]{:S(2)}, u32[]{:S(2)}) collective-permute-start(bf16[16,2048]{1,0:T(8,128)(2,1)} %fusion.5), channel_id=1, source_target_pairs={{0,16},{8,24},{16,0},{24,8},{1,17},{9,25},{17,1},{25,9},{2,18},{10... | collective-permute-start | bytes 196616 | tf_op jit(solution)/shard_map/ppermute | solution.py:276
  168.4 1.0 copy-start.13
  169.4 1.0 copy-start.15
  170.4 14.5 %copy-start.23 = (f32[2,16,2048]{2,1,0:T(8,128)S(1)}, f32[2,16,2048]{2,1,0:T(8,128)}, u32[]{:S(2)}) copy-start(f32[2,16,2048]{2,1,0:T(8,128)} %copy-done.22) | copy-start | bytes 786436
  182.5 7.0 %collective-permute-start.17 = (f32[49,512]{1,0:T(8,128)S(1)}, f32[49,512]{1,0:T(8,128)S(1)}, u32[]{:S(2)}, u32[]{:S(2)}) collective-permute-start(f32[49,512]{1,0:T(8,128)S(1)} %add.114), channel_id=1, source_target_pairs={{0,16},{8,24},{16,0},{24,8},{1,17},{9,25},{17,1},{25,9},{2,18},{10... | collective-permute-start | bytes 301064 | tf_op jit(solution)/shard_map/ppermute | solution.py:276
